TPU v7x, 32 devices: a whole 2x2x4 slice. The times are simulated.
32 devices in a mesh: seq: 8 (over y, x, core), head: 4 (over z).
Axes of the slice: x: 2, y: 2, z: 4, core: 2. Of those that a mesh axis runs over, the one named last changes fastest.
Arguments:
- queries: bfloat16 [3072, 3072], P('seq', 'head'), may hold values from -8 to 8
- key_states: bfloat16 [3072, 3072], P('seq', 'head'), may hold values from -8 to 8
- value_states: bfloat16 [3072, 3072], P('seq', 'head'), may hold values from -6 to 6
- block_lists: int32 [24, 4], replicated, may hold values from 0 to 23, as said below
- out_weight: bfloat16 [3072, 3072], P('head'), may hold values from -0.15625 to 0.15625
- out_grad: bfloat16 [3072, 3072], P('seq', 'head'), may hold values from -6 to 6
Outputs:
- attended: bfloat16 [3072, 3072], P('seq', 'head')
- query_grad: bfloat16 [3072, 3072], P('seq', 'head')
- key_grad: bfloat16 [3072, 3072], P('seq', 'head')
- value_grad: bfloat16 [3072, 3072], P('seq', 'head')
Inputs may be any that keep to these rules, and one draw needn't show every extreme that they name: `block_lists`: row r names 4 different blocks, among them block r itself; 2 of them lie in r's own group of 3 blocks and 2 in other groups. Of each group's blocks at most two are named by rows of other groups, and the rows of one group name at most one block of any other group.
All inputs are finite; a program needn't handle non-finite values.
Results may differ from a plain program's by a relative error of at most 0.035.
Values may be sent and summed in bfloat16 or wider, within the bound.
A program may use at most 192 MiB of HBM per device.

v0:
```python
import functools
import math

import jax
import jax.numpy as jnp
from jax import lax
from jax.experimental import pallas as pl
from jax.experimental.pallas import tpu as pltpu
from jax.sharding import PartitionSpec as P

HD = 128
BLK = 128
K_SEL = 4
MESH = pl.DeviceIdType.MESH
BF = jnp.bfloat16
F32 = jnp.float32


def dot_nn(a, b):
    return lax.dot_general(a, b, (((1,), (0,)), ((), ())), preferred_element_type=F32)


def dot_nt(a, b):
    return lax.dot_general(a, b, (((1,), (1,)), ((), ())), preferred_element_type=F32)


def dot_tn(a, b):
    return lax.dot_general(a, b, (((0,), (0,)), ((), ())), preferred_element_type=F32)


def kernel(
    n_seq, n_head, lists_hbm, q_hbm, k_hbm, v_hbm, og, w_hbm,
    att_o, dq_o, dk_o, dv_o,
    q, k, v, table_k, table_v, k_send, v_send, w, og_all, p_scr, ds_scr, attn, part_send, from_below, from_above,
    ga_acc, ga, ret_send, ret_recv, acc_k, acc_v, lists, slot_s, asked_s, idx_s,
    load_sem, og_up, og_down, og_recv, k_ssem, k_rsem, v_ssem, v_rsem,
    pt_ssem, below_sem, above_sem, rt_ssem, rt_rsem,
):
    cells, width = q.shape
    blocks = cells // BLK
    heads = width // HD
    scale = 1.0 / math.sqrt(HD)
    s_me = lax.axis_index("seq")
    z = lax.axis_index("head")

    barrier = pltpu.get_barrier_semaphore()
    for o in range(1, n_head):
        pl.semaphore_signal(
            barrier, inc=1, device_id={"head": lax.rem(z + o, n_head)}, device_id_type=MESH
        )
    for o in range(1, n_seq):
        pl.semaphore_signal(
            barrier, inc=1, device_id={"seq": lax.rem(s_me + o, n_seq)}, device_id_type=MESH
        )
    loads = [
        pltpu.make_async_copy(src, dst, load_sem.at[i])
        for i, (src, dst) in enumerate(
            ((lists_hbm, lists), (k_hbm, k), (v_hbm, v), (og, og_all.at[z]), (q_hbm, q), (w_hbm, w))
        )
    ]
    for load in loads:
        load.start()
    for load in loads[:3]:
        load.wait()

    def stage(i, carry):
        d = lax.rem(s_me + n_seq - i, n_seq)
        asked = jnp.int32(0)
        for r in range(blocks):
            for c in range(K_SEL):
                entry = lists[c, d * blocks + r] - s_me * blocks
                asked = jnp.where((entry >= 0) & (entry < blocks), entry, asked)
        asked_s[d] = asked
        k_send[d] = k[asked]
        v_send[d] = v[asked]
        return carry

    lax.fori_loop(1, n_seq, stage, 0)
    pl.semaphore_wait(barrier, n_head - 1 + n_seq - 1)

    def chunk(c):
        return pl.ds(pl.multiple_of(c * BLK, BLK), BLK)

    def og_copy(shard, c, up, own):
        src = og.at[chunk(c), :] if own else og_all.at[shard, chunk(c), :]
        return pltpu.make_async_remote_copy(
            src_ref=src,
            dst_ref=og_all.at[shard, chunk(c), :],
            send_sem=(og_up if up else og_down).at[shard, c],
            recv_sem=og_recv.at[shard, c],
            device_id={"head": z + 1 if up else z - 1},
            device_id_type=MESH,
        )

    for c in range(blocks):
        @pl.when(z < n_head - 1)
        def _():
            og_copy(z, c, True, True).start()

        @pl.when(z > 0)
        def _():
            og_copy(z, c, False, True).start()

    def k_copy(d):
        return pltpu.make_async_remote_copy(
            src_ref=k_send.at[d],
            dst_ref=table_k.at[s_me],
            send_sem=k_ssem.at[d],
            recv_sem=k_rsem.at[s_me],
            device_id={"seq": d},
            device_id_type=MESH,
        )

    def v_copy(d):
        return pltpu.make_async_remote_copy(
            src_ref=v_send.at[d],
            dst_ref=table_v.at[s_me],
            send_sem=v_ssem.at[d],
            recv_sem=v_rsem.at[s_me],
            device_id={"seq": d},
            device_id_type=MESH,
        )

    def send(copy):
        def one(i, carry):
            copy(lax.rem(s_me + n_seq - i, n_seq)).start()
            return carry

        lax.fori_loop(1, n_seq, one, 0)

    send(k_copy)
    send(v_copy)

    for b in range(blocks):
        table_k[n_seq + b] = k[b]
        table_v[n_seq + b] = v[b]
        for c in range(K_SEL):
            entry = lists[c, s_me * blocks + b]
            near = entry - s_me * blocks
            own = (near >= 0) & (near < blocks)
            slot_s[b * K_SEL + c] = jnp.where(own, n_seq + near, lax.div(entry, jnp.int32(blocks)))
        ds_scr[b, K_SEL] = jnp.zeros((BLK, BLK), BF)
        for h in range(heads):
            p_scr[h, b, K_SEL] = jnp.zeros((BLK, BLK), BF)

    def fill_index(t, carry):
        for b in range(blocks):
            place = jnp.int32(K_SEL)
            for c in range(K_SEL):
                place = jnp.where(slot_s[b * K_SEL + c] == t, c, place)
            idx_s[t * blocks + b] = place
        return carry

    lax.fori_loop(0, n_seq + blocks, fill_index, 0)

    for load in loads[3:]:
        load.wait()

    def w_cols(shard):
        return w[:, pl.ds(pl.multiple_of(shard * width, width), width)]

    ga_acc[...] = dot_nt(og_all[z], w_cols(z))

    def og_round(step, carry):
        def one(c, inner):
            @pl.when(z - step >= 0)
            def _():
                og_copy(z - step, c, True, False).wait_recv()

                @pl.when(z < n_head - 1)
                def _():
                    og_copy(z - step, c, True, False).start()

            @pl.when(z + step < n_head)
            def _():
                og_copy(z + step, c, False, False).wait_recv()

                @pl.when(z > 0)
                def _():
                    og_copy(z + step, c, False, False).start()

            return inner

        lax.fori_loop(0, blocks, one, 0)

        @pl.when(z - step >= 0)
        def _():
            ga_acc[...] += dot_nt(og_all[z - step], w_cols(z - step))

        @pl.when(z + step < n_head)
        def _():
            ga_acc[...] += dot_nt(og_all[z + step], w_cols(z + step))

        return carry

    lax.fori_loop(1, n_head - 1, og_round, 0)

    def landed(buffer, table, ssem, rsem):
        def one(i, carry):
            src = lax.rem(s_me + i, n_seq)
            pltpu.make_async_remote_copy(
                src_ref=buffer.at[src],
                dst_ref=table.at[src],
                send_sem=ssem.at[src],
                recv_sem=rsem.at[src],
                device_id={"seq": src},
                device_id_type=MESH,
            ).wait_recv()
            return carry

        lax.fori_loop(1, n_seq, one, 0)

    def picked(table, b, h):
        cols = pl.ds(pl.multiple_of(h * HD, HD), HD)
        return jnp.concatenate(
            [table[slot_s[b * K_SEL + c], :, cols] for c in range(K_SEL)], axis=0
        )

    landed(k_send, table_k, k_ssem, k_rsem)

    def weigh(h, carry):
        cols = pl.ds(pl.multiple_of(h * HD, HD), HD)
        for b in range(blocks):
            rows = slice(b * BLK, (b + 1) * BLK)
            scores = dot_nt(picked(table_k, b, h), q[rows, cols]) * scale
            top = jnp.max(scores, axis=0, keepdims=True)
            weights = jnp.exp(scores - top)
            total = jnp.sum(weights, axis=0, keepdims=True)
            probs = (weights * (1.0 / total)).astype(BF)
            for c in range(K_SEL):
                p_scr[h, b, c] = probs[c * BLK:(c + 1) * BLK]
        return carry

    lax.fori_loop(0, heads, weigh, 0)

    def probs_of(h, b):
        return jnp.concatenate([p_scr[h, b, c] for c in range(K_SEL)], axis=0)

    landed(v_send, table_v, v_ssem, v_rsem)

    def attend(h, carry):
        cols = pl.ds(pl.multiple_of(h * HD, HD), HD)
        for b in range(blocks):
            rows = slice(b * BLK, (b + 1) * BLK)
            attn[rows, cols] = dot_tn(probs_of(h, b), picked(table_v, b, h)).astype(BF)
        return carry

    lax.fori_loop(0, heads, attend, 0)

    def part_copy(d, c, up):
        landing = from_below if up else from_above
        return pltpu.make_async_remote_copy(
            src_ref=part_send.at[d, chunk(c), :],
            dst_ref=landing.at[d, chunk(c), :],
            send_sem=pt_ssem.at[d, c],
            recv_sem=(below_sem if up else above_sem).at[d, c],
            device_id={"head": z + 1 if up else z - 1},
            device_id_type=MESH,
        )

    def project(i, carry):
        last = lax.div(z, n_head - 1)
        d = last * i + (1 - last) * (n_head - 1 - i)
        part_send[d] = dot_nn(attn[...], w_cols(d)).astype(BF)
        for c in range(blocks):
            @pl.when((z == 0) & (d > 0))
            def _():
                part_copy(d, c, True).start()

            @pl.when((z == n_head - 1) & (d < n_head - 1))
            def _():
                part_copy(d, c, False).start()

        return carry

    lax.fori_loop(0, n_head, project, 0)

    og_round(n_head - 1, 0)
    ga[...] = ga_acc[...].astype(BF)

    def ret_copy(h, d):
        return pltpu.make_async_remote_copy(
            src_ref=ret_send.at[h, d],
            dst_ref=ret_recv.at[h, s_me],
            send_sem=rt_ssem.at[h, d],
            recv_sem=rt_rsem.at[h, s_me],
            device_id={"seq": d},
            device_id_type=MESH,
        )

    def backward(h, carry):
        cols = pl.ds(pl.multiple_of(h * HD, HD), HD)
        for b in range(blocks):
            rows = slice(b * BLK, (b + 1) * BLK)
            probs = probs_of(h, b).astype(F32)
            grad_prob = dot_nt(picked(table_v, b, h), ga[rows, cols])
            delta = jnp.sum(probs * grad_prob, axis=0, keepdims=True)
            grad_score = (probs * (grad_prob - delta)).astype(BF)
            for c in range(K_SEL):
                ds_scr[b, c] = grad_score[c * BLK:(c + 1) * BLK]
            dq_o[rows, cols] = (dot_tn(grad_score, picked(table_k, b, h)) * scale).astype(BF)
        q_cols = q[:, cols]
        g_cols = ga[:, cols]

        def terms(t):
            places = [idx_s[t * blocks + b] for b in range(blocks)]
            ds_t = jnp.concatenate([ds_scr[b, places[b]] for b in range(blocks)], axis=1)
            p_t = jnp.concatenate([p_scr[h, b, places[b]] for b in range(blocks)], axis=1)
            return dot_nn(ds_t, q_cols) * scale, dot_nn(p_t, g_cols)

        for i in range(1, n_seq):
            d = lax.rem(s_me + n_seq - i, n_seq)
            key_part, value_part = terms(d)
            ret_send[h, d, :, :HD] = key_part.astype(BF)
            ret_send[h, d, :, HD:] = value_part.astype(BF)
            ret_copy(h, d).start()
        for b in range(blocks):
            rows = slice(b * BLK, (b + 1) * BLK)
            acc_k[rows, cols], acc_v[rows, cols] = terms(n_seq + b)
        return carry

    lax.fori_loop(0, heads, backward, 0)

    def hand_on(tick, carry):
        u = tick - z

        @pl.when((z > 0) & (u >= 0) & (u < blocks * (n_head - 1 - z)))
        def _():
            d = n_head - 1 - u // blocks
            c = lax.rem(u, blocks)
            part_copy(d, c, True).wait_recv()
            part_send[d, chunk(c), :] = (
                part_send[d, chunk(c), :].astype(F32) + from_below[d, chunk(c), :].astype(F32)
            ).astype(BF)
            part_copy(d, c, True).start()

        t = tick - (n_head - 1 - z)

        @pl.when((z < n_head - 1) & (t >= 0) & (t < blocks * z))
        def _():
            d = t // blocks
            c = lax.rem(t, blocks)
            part_copy(d, c, False).wait_recv()
            part_send[d, chunk(c), :] = (
                part_send[d, chunk(c), :].astype(F32) + from_above[d, chunk(c), :].astype(F32)
            ).astype(BF)
            part_copy(d, c, False).start()

        return carry

    lax.fori_loop(1, blocks * (n_head - 1) + n_head, hand_on, 0)

    def collect(h, carry):
        cols = pl.ds(pl.multiple_of(h * HD, HD), HD)

        def ret_wait(i, inner):
            src = lax.rem(s_me + i, n_seq)
            pltpu.make_async_remote_copy(
                src_ref=ret_send.at[h, src],
                dst_ref=ret_recv.at[h, src],
                send_sem=rt_ssem.at[h, src],
                recv_sem=rt_rsem.at[h, src],
                device_id={"seq": src},
                device_id_type=MESH,
            ).wait_recv()
            return inner

        lax.fori_loop(1, n_seq, ret_wait, 0)
        for b in range(blocks):
            rows = slice(b * BLK, (b + 1) * BLK)
            key_sum = acc_k[rows, cols]
            value_sum = acc_v[rows, cols]
            for i in range(1, n_seq):
                src = lax.rem(s_me + i, n_seq)
                flag = jnp.where(asked_s[src] == b, 1.0, 0.0)
                key_sum += flag * ret_recv[h, src, :, :HD].astype(F32)
                value_sum += flag * ret_recv[h, src, :, HD:].astype(F32)
            dk_o[rows, cols] = key_sum.astype(BF)
            dv_o[rows, cols] = value_sum.astype(BF)
        return carry

    lax.fori_loop(0, heads, collect, 0)

    for c in range(blocks):
        rows = slice(c * BLK, (c + 1) * BLK)
        ga_acc[rows, :] = part_send[z, rows, :].astype(F32)

        @pl.when(z > 0)
        def _():
            part_copy(z, c, True).wait_recv()
            ga_acc[rows, :] += from_below[z, rows, :].astype(F32)

        @pl.when(z < n_head - 1)
        def _():
            part_copy(z, c, False).wait_recv()
            ga_acc[rows, :] += from_above[z, rows, :].astype(F32)

        att_o[rows, :] = ga_acc[rows, :].astype(BF)

    def og_drain(c, carry):
        for step in range(n_head - 1):
            @pl.when((z - step >= 0) & (z < n_head - 1))
            def _():
                og_copy(z - step, c, True, False).wait_send()

            @pl.when((z + step < n_head) & (z > 0))
            def _():
                og_copy(z + step, c, False, False).wait_send()

        for d in range(n_head):
            @pl.when(z != d)
            def _():
                part_copy(d, c, True).wait_send()

        return carry

    lax.fori_loop(0, blocks, og_drain, 0)

    def seq_drain(i, carry):
        d = lax.rem(s_me + i, n_seq)
        k_copy(d).wait_send()
        v_copy(d).wait_send()

        def one(h, inner):
            ret_copy(h, d).wait_send()
            return inner

        return lax.fori_loop(0, heads, one, carry)

    lax.fori_loop(1, n_seq, seq_drain, 0)


def write_out(a0, a1, a2, a3, o0, o1, o2, o3, sems):
    copies = []
    for i, (src, dst) in enumerate(((a0, o0), (a1, o1), (a2, o2), (a3, o3))):
        for c in range(src.shape[0] // BLK):
            rows = pl.ds(c * BLK, BLK)
            copies.append(pltpu.make_async_copy(src.at[rows, :], dst.at[rows, :], sems.at[i, c]))
    for copy in copies:
        copy.start()
    for copy in copies:
        copy.wait()


def local(queries, key_states, value_states, block_lists, out_weight, out_grad):
    n_seq = lax.axis_size("seq")
    n_head = lax.axis_size("head")
    cells, width = queries.shape
    blocks = cells // BLK
    heads = width // HD
    slots = n_seq + blocks
    vmem = pl.BlockSpec(memory_space=pltpu.VMEM)
    main = pl.BlockSpec(memory_space=pltpu.HBM)
    sem = pltpu.SemaphoreType.DMA
    out = jax.ShapeDtypeStruct((cells, width), BF)
    held = pltpu.VMEM((cells, width), BF)
    results = pl.pallas_call(
        functools.partial(kernel, n_seq, n_head),
        out_shape=(held, held, held, held),
        in_specs=[
            main, main, main, main, main, main,
        ],
        out_specs=(vmem, vmem, vmem, vmem),
        scratch_shapes=[
            pltpu.VMEM((cells, width), BF),
            pltpu.VMEM((blocks, BLK, width), BF),
            pltpu.VMEM((blocks, BLK, width), BF),
            pltpu.VMEM((slots, BLK, width), BF),
            pltpu.VMEM((slots, BLK, width), BF),
            pltpu.VMEM((n_seq, BLK, width), BF),
            pltpu.VMEM((n_seq, BLK, width), BF),
            pltpu.VMEM(out_weight.shape, BF),
            pltpu.VMEM((n_head, cells, width), BF),
            pltpu.VMEM((heads, blocks, K_SEL + 1, BLK, BLK), BF),
            pltpu.VMEM((blocks, K_SEL + 1, BLK, BLK), BF),
            pltpu.VMEM((cells, width), BF),
            pltpu.VMEM((n_head, cells, width), BF),
            pltpu.VMEM((n_head, cells, width), BF),
            pltpu.VMEM((n_head, cells, width), BF),
            pltpu.VMEM((cells, width), F32),
            pltpu.VMEM((cells, width), BF),
            pltpu.VMEM((heads, n_seq, BLK, 2 * HD), BF),
            pltpu.VMEM((heads, n_seq, BLK, 2 * HD), BF),
            pltpu.VMEM((cells, width), F32),
            pltpu.VMEM((cells, width), F32),
            pltpu.SMEM(block_lists.shape[::-1], jnp.int32),
            pltpu.SMEM((blocks * K_SEL,), jnp.int32),
            pltpu.SMEM((n_seq,), jnp.int32),
            pltpu.SMEM((slots * blocks,), jnp.int32),
            sem((6,)), sem((n_head, blocks)), sem((n_head, blocks)), sem((n_head, blocks)),
            sem((n_seq,)), sem((n_seq,)), sem((n_seq,)), sem((n_seq,)),
            sem((n_head, blocks)), sem((n_head, blocks)), sem((n_head, blocks)),
            sem((heads, n_seq)), sem((heads, n_seq)),
        ],
        compiler_params=pltpu.CompilerParams(
            collective_id=0, has_side_effects=True, vmem_limit_bytes=56 * 1024 * 1024
        ),
        cost_estimate=pl.CostEstimate(
            flops=8 * 10**9, bytes_accessed=20 * 10**6, transcendentals=10**6
        ),
    )(
        block_lists.T,
        queries,
        key_states.reshape(blocks, BLK, width),
        value_states.reshape(blocks, BLK, width),
        out_grad,
        out_weight,
    )
    return pl.pallas_call(
        write_out,
        out_shape=(out, out, out, out),
        in_specs=[vmem] * 4,
        out_specs=(main,) * 4,
        scratch_shapes=[sem((4, blocks))],
    )(*results)


def solution(mesh):
    in_specs = (
        P("seq", "head"),
        P("seq", "head"),
        P("seq", "head"),
        P(),
        P("head", None),
        P("seq", "head"),
    )
    out_specs = (P("seq", "head"), P("seq", "head"), P("seq", "head"), P("seq", "head"))
    return jax.shard_map(local, mesh=mesh, in_specs=in_specs, out_specs=out_specs, check_vma=False)
```

profile of v0, /device:TPU:8, one launch (start us, length us, event | category | flops | bytes accessed | tf_op | source)
XLA Modules:
  0.0 94.2 jit_solution(9122227093736952755)
XLA Ops:
  0.6 87.1 %shard_map.93 = (bf16[384,768]{1,0:T(8,128)(2,1)S(1)}, bf16[384,768]{1,0:T(8,128)(2,1)S(1)}, bf16[384,768]{1,0:T(8,128)(2,1)S(1)}, bf16[384,768]{1,0:T(8,128)(2,1)S(1)}) custom-call(s32[4,24]{1,0:T(4,128)} %bitcast.5, bf16[384,768]{1,0:T(8,128)(2,1)} %q_hbm.1, bf16[3,128,768]{2,1,0:T(8,128)(2,1)} %bitcast.3, bf16[3,128,768]{2,1,0:T(8,128)(2,1)} %bitcast.4, ...), custom_call_target="tpu_custom_call" | custom-call | flops 8000000000 | bytes 20000000 | tf_op jit(solution)/shard_map/pallas_call | solution.py:457
  87.7 0.0 copy-start
  87.8 0.8 copy-done
  88.6 0.0 copy-start.1
  88.6 0.8 copy-done.1
  89.4 0.0 copy-start.2
  89.4 0.8 copy-done.2
  90.3 0.0 copy-start.3
  90.3 0.8 copy-done.3
  91.1 3.1 %shard_map.94 = (bf16[384,768]{1,0:T(8,128)(2,1)}, bf16[384,768]{1,0:T(8,128)(2,1)}, bf16[384,768]{1,0:T(8,128)(2,1)}, bf16[384,768]{1,0:T(8,128)(2,1)}) custom-call(bf16[384,768]{1,0:T(8,128)(2,1)} %copy-done, bf16[384,768]{1,0:T(8,128)(2,1)} %copy-done.1, bf16[384,768]{1,0:T(8,128)(2,1)} %copy-done.2, bf16[384,768]{1,0:T(8,128)(2,1)} %copy-done.3), custom_call_target="tpu_custom_call" | custom-call | tf_op jit(solution)/shard_map/pallas_call | solution.py:509
Async XLA Ops:
  87.7 0.8 copy-start
  88.6 0.8 copy-start.1
  89.4 0.8 copy-start.2
  90.3 0.8 copy-start.3
where the time goes:
time: 94.3 us; the launch traced here: 94.2 us
  Pallas kernels  90.2 us (96%)
  local copies, waits for them, and re-layouts  3.35 us (4%)
    pallas_call x1, Pallas kernels, local(): pl.pallas_call(functools.partial(kernel, n_seq, n_head), out_shape=(held,...  87.1 us
    unnamed x8, local copies, waits for them, and re-layouts  3.35 us
    pallas_call x1, Pallas kernels, local(): pl.pallas_call(write_out, out_shape=(out, out, out, out), in_specs=[vmem]...  3.09 us

commit v1 on v0

--- a/solution.py
+++ b/solution.py
@@ -512,6 +512,7 @@
         in_specs=[vmem] * 4,
         out_specs=(main,) * 4,
         scratch_shapes=[sem((4, blocks))],
+        compiler_params=pltpu.CompilerParams(vmem_limit_bytes=8 * 1024 * 1024),
     )(*results)
 
 

time: 94.3 us -> 89.4 us (0.948)
  local copies, waits for them, and re-layouts: 3.35 us -> 0 us
  Pallas kernels: 90.2 us -> 88.6 us
    unnamed x8 -> x0, local copies, waits for them, and re-layouts: 3.35 us -> none
    pallas_call x1, Pallas kernels: 3.09 us -> 1.49 us  [local(): pl.pallas_call(write_out, out_shape=(out, out, out, out), in_specs=[vmem]...]
where the time goes in v1:
time: 89.4 us; the launch traced here: 89.2 us
  Pallas kernels  88.6 us (99%)
    pallas_call x1, Pallas kernels, local(): pl.pallas_call(functools.partial(kernel, n_seq, n_head), out_shape=(held,...  87.1 us

profile of v1, /device:TPU:8, one launch (start us, length us, event | category | flops | bytes accessed | tf_op | source)
XLA Modules:
  0.0 89.2 jit_solution(13276635330821459443)
XLA Ops:
  0.6 87.1 %shard_map.93 = (bf16[384,768]{1,0:T(8,128)(2,1)S(1)}, bf16[384,768]{1,0:T(8,128)(2,1)S(1)}, bf16[384,768]{1,0:T(8,128)(2,1)S(1)}, bf16[384,768]{1,0:T(8,128)(2,1)S(1)}) custom-call(s32[4,24]{1,0:T(4,128)} %bitcast.5, bf16[384,768]{1,0:T(8,128)(2,1)} %q_hbm.1, bf16[3,128,768]{2,1,0:T(8,128)(2,1)} %bitcast.3, bf16[3,128,768]{2,1,0:T(8,128)(2,1)} %bitcast.4, ...), custom_call_target="tpu_custom_call" | custom-call | flops 8000000000 | bytes 20000000 | tf_op jit(solution)/shard_map/pallas_call | solution.py:457
  87.7 1.5 %shard_map.94 = (bf16[384,768]{1,0:T(8,128)(2,1)}, bf16[384,768]{1,0:T(8,128)(2,1)}, bf16[384,768]{1,0:T(8,128)(2,1)}, bf16[384,768]{1,0:T(8,128)(2,1)}) custom-call(bf16[384,768]{1,0:T(8,128)(2,1)S(1)} %get-tuple-element.8.a0, bf16[384,768]{1,0:T(8,128)(2,1)S(1)} %get-tuple-element.9.a1, bf16[384,768]{1,0:T(8,128)(2,1)S(1)} %get-tuple-element.10.a2, ...), custom_call_target="tpu_custom_call" | custom-call | tf_op jit(solution)/shard_map/pallas_call | solution.py:509
